TPU v7x, 256 devices: a whole 4x4x8 slice. The times are simulated.
256 devices in a mesh: gx: 64 (over z, x, core), gy: 4 (over y).
Axes of the slice: x: 4, y: 4, z: 8, core: 2. Of those that a mesh axis runs over, the one named last changes fastest.
Arguments:
- embeddings: bfloat16 [262144, 768], P(('gx', 'gy')), may hold values from -12 to 12
- clusters: int32 [262144], P(('gx', 'gy')), may hold values from 0 to 511, as said below
- priorities: int32 [262144], P(('gx', 'gy')), may hold values from 0 to 262143, each once
Outputs:
- best_similarity: float32 [262144], P(('gx', 'gy'))
Inputs may be any that keep to these rules, and one draw needn't show every extreme that they name: For every o, the rows of one device name the 2 clusters c with c // 2 == o at most 6 times together; one cluster, drawn from the seed, is named exactly 6 times by the rows of every device. `priorities`: all distinct.
All inputs are finite; a program needn't handle non-finite values.
Results may differ from a plain program's by a relative error of at most 0.0003.
Values may be sent and summed in bfloat16 or wider, within the bound.
No kernel may reach another device: no remote copies, remote signals or barrier semaphores. Data moves between devices by JAX's collectives and lax.ppermute only.
A program may use at most 128 MiB of HBM per device.

v0:
```python
import jax
import jax.numpy as jnp
from jax import lax
from jax.sharding import PartitionSpec as P

CLUS_DEV = 2


norm_eps = 1e-06
dead_key = 1073741824


def inverse_norm(values):
    wide = values.astype(jnp.float32)
    return lax.rsqrt(jnp.sum(wide * wide, axis=-1) + norm_eps)


def cluster_max(
    query_rows, query_order, query_label, query_scale, key_rows, key_order, key_label, running
):
    scores = jnp.einsum("cqd,ckd->cqk", query_rows, key_rows, preferred_element_type=jnp.float32)
    scores = scores * query_scale[:, :, None] * inverse_norm(key_rows)[:, None, :]
    earlier = key_order[:, None, :] < query_order[:, :, None]
    alike = key_label[:, None, :] == query_label[:, :, None]
    return jnp.maximum(running, jnp.max(jnp.where(earlier & alike, scores, -1.0), axis=2))


def shards(embeddings, clusters, priorities):
    row_count, width = embeddings.shape
    count_x = lax.axis_size("gx")
    count_y = lax.axis_size("gy")
    device_count = count_x * count_y
    cluster_total = CLUS_DEV * device_count
    slots = 3 * row_count // (2 * device_count)
    position = jnp.arange(row_count, dtype=jnp.int32)
    same_before = (clusters[:, None] == clusters[None, :]) & (position[None, :] < position[:, None])
    target = clusters * slots + jnp.sum(same_before.astype(jnp.int32), axis=1)
    outgoing = (
        jnp.zeros((cluster_total * slots, width), embeddings.dtype).at[target].set(embeddings)
    )
    out_order = jnp.full((cluster_total * slots,), dead_key, jnp.int32).at[target].set(priorities)
    out_label = jnp.full((cluster_total * slots,), -1, jnp.int32).at[target].set(clusters)
    outgoing = outgoing.reshape(cluster_total, slots, width)
    out_order = out_order.reshape(cluster_total, slots)
    out_label = out_label.reshape(cluster_total, slots)
    owned, owned_order, owned_label = (
        lax.all_to_all(
            lax.all_to_all(outgoing, "gx", split_axis=0, concat_axis=1, tiled=True),
            "gy",
            split_axis=0,
            concat_axis=1,
            tiled=True,
        ),
        lax.all_to_all(
            lax.all_to_all(out_order, "gx", split_axis=0, concat_axis=1, tiled=True),
            "gy",
            split_axis=0,
            concat_axis=1,
            tiled=True,
        ),
        lax.all_to_all(
            lax.all_to_all(out_label, "gx", split_axis=0, concat_axis=1, tiled=True),
            "gy",
            split_axis=0,
            concat_axis=1,
            tiled=True,
        ),
    )
    start_best = jnp.full(owned_order.shape, -1.0, jnp.float32)
    results = cluster_max(
        owned,
        owned_order,
        owned_label,
        inverse_norm(owned),
        owned,
        owned_order,
        owned_label,
        start_best,
    )
    local_groups = results.shape[0]
    arranged = results.reshape(local_groups, count_y, count_x, slots).transpose(0, 2, 1, 3)
    received = lax.all_to_all(
        lax.all_to_all(arranged, "gx", split_axis=1, concat_axis=0, tiled=True),
        "gy",
        split_axis=2,
        concat_axis=0,
        tiled=True,
    )
    returned = received.reshape(count_y, count_x, local_groups, slots).transpose(1, 0, 2, 3)
    return returned.reshape(-1)[target]


def solution(mesh):
    in_specs = (P(("gx", "gy"), None), P(("gx", "gy")), P(("gx", "gy")))
    out_specs = P(("gx", "gy"))
    return jax.shard_map(shards, mesh=mesh, in_specs=in_specs, out_specs=out_specs, check_vma=False)
```

profile of v0, /device:TPU:1, one launch (start us, length us, event | category | flops | bytes accessed | tf_op | source)
XLA Modules:
  0.0 335.7 jit_solution(7528284845405142965)
XLA Ops:
  0.0 1.3 convert_reduce_fusion
  2.0 4.5 %scatter_custom_fusion = s32[3072]{0:T(1024)S(1)} fusion(s32[1024]{0:T(1024)S(1)} %get-tuple-element.6, s32[1024]{0:T(1024)} %param.5, s32[]{:T(128)} %constant.10.clone.1), kind=kCustom, calls=%fused_computation.16 | custom fusion | bytes 12800 | tf_op jit(solution)/shard_map/scatter | solution.py:41
  6.5 0.9 all_to_all.98
  7.4 13.0 %all-to-all-start = ((s32[64,8,6]{2,1,0:T(8,128)}), s32[64,8,6]{2,1,0:T(8,128)S(1)}, u32[]{:S(2)}, u32[]{:S(2)}) async-start(s32[64,8,6]{2,1,0:T(8,128)} %all_to_all.98), calls=%async_computation | async-start | bytes 524288 | tf_op jit(solution)/shard_map/all_to_all | solution.py:55
  20.4 8.8 %scatter_custom_fusion.2 = bf16[3072,768]{1,0:T(8,128)(2,1)} fusion(s32[1024]{0:T(1024)S(1)} %get-tuple-element.6, bf16[1024,768]{1,0:T(8,128)(2,1)} %param.3, bf16[]{:T(256)} %constant.3.clone.1), kind=kCustom, calls=%fused_computation.9 | custom fusion | bytes 4719104 | tf_op jit(solution)/shard_map/scatter | solution.py:39
  29.2 8.5 %reshape.60 = bf16[512,6,768]{2,1,0:T(8,128)(2,1)} reshape(bf16[3072,768]{1,0:T(8,128)(2,1)} %scatter_custom_fusion.2) | data formatting | bytes 9437184 | tf_op jit(solution)/shard_map/reshape | solution.py:43
  37.7 10.5 %all-to-all-start.4 = ((bf16[512,6,768]{2,1,0:T(8,128)(2,1)}), bf16[512,6,768]{2,1,0:T(8,128)(2,1)}, u32[]{:S(2)}, u32[]{:S(2)}) async-start(bf16[512,6,768]{2,1,0:T(8,128)(2,1)} %reshape.60), calls=%async_computation.4 | async-start | bytes 12582912 | tf_op jit(solution)/shard_map/all_to_all | solution.py:48
  48.2 4.5 %scatter_custom_fusion.1 = s32[3072]{0:T(1024)S(1)} fusion(s32[1024]{0:T(1024)S(1)} %get-tuple-element.6, s32[1024]{0:T(1024)} %param.4, s32[]{:T(128)} %constant.2.clone.1), kind=kCustom, calls=%fused_computation.14 | custom fusion | bytes 12800 | tf_op jit(solution)/shard_map/scatter | solution.py:42
  52.7 0.9 all_to_all.104
  53.6 133.1 %all-to-all-done.4 = bf16[512,6,768]{2,1,0:T(8,128)(2,1)} async-done(((bf16[512,6,768]{2,1,0:T(8,128)(2,1)}), bf16[512,6,768]{2,1,0:T(8,128)(2,1)}, u32[]{:S(2)}, u32[]{:S(2)}) %all-to-all-start.4) | async-done | bytes 4718624 | tf_op jit(solution)/shard_map/all_to_all | solution.py:48
  186.7 8.3 %all-to-all-start.2 = ((s32[64,8,6]{2,1,0:T(8,128)}), s32[64,8,6]{2,1,0:T(8,128)S(1)}, u32[]{:S(2)}, u32[]{:S(2)}) async-start(s32[64,8,6]{2,1,0:T(8,128)} %all_to_all.104), calls=%async_computation.2 | async-start | bytes 524288 | tf_op jit(solution)/shard_map/all_to_all | solution.py:62
  195.0 4.1 %copy.32 = bf16[64,8,6,768]{3,1,2,0:T(8,128)(2,1)S(1)} copy(bf16[64,8,6,768]{3,2,1,0:T(8,128)(2,1)} %bitcast.8) | data formatting | bytes 9437184 | tf_op jit(solution)/shard_map/all_to_all | solution.py:48
  199.2 3.1 copy.33
  202.3 5.9 %all-to-all-done.2 = s32[64,8,6]{2,1,0:T(8,128)S(1)} async-done(((s32[64,8,6]{2,1,0:T(8,128)}), s32[64,8,6]{2,1,0:T(8,128)S(1)}, u32[]{:S(2)}, u32[]{:S(2)}) %all-to-all-start.2) | async-done | bytes 12320 | tf_op jit(solution)/shard_map/all_to_all | solution.py:62
  208.2 4.9 %all-to-all-start.5 = ((bf16[8,384,768]{2,1,0:T(8,128)(2,1)}), bf16[8,384,768]{2,1,0:T(8,128)(2,1)}, u32[]{:S(2)}, u32[]{:S(2)}) async-start(bf16[8,384,768]{2,1,0:T(8,128)(2,1)} %copy.33), calls=%async_computation.5 | async-start | bytes 9437184 | tf_op jit(solution)/shard_map/all_to_all | solution.py:47
  214.8 52.7 %all-to-all-done.5 = bf16[8,384,768]{2,1,0:T(8,128)(2,1)} async-done(((bf16[8,384,768]{2,1,0:T(8,128)(2,1)}), bf16[8,384,768]{2,1,0:T(8,128)(2,1)}, u32[]{:S(2)}, u32[]{:S(2)}) %all-to-all-start.5) | async-done | bytes 4718624 | tf_op jit(solution)/shard_map/all_to_all | solution.py:47
  267.5 3.2 all-to-all-start.1
  270.8 3.3 multiply_reduce_fusion
  274.9 3.4 %all-to-all-start.3 = ((s32[4,2,384]{2,1,0:T(2,128)}), s32[4,2,384]{2,1,0:T(2,128)S(1)}, u32[]{:S(2)}, u32[]{:S(2)}) async-start(s32[4,2,384]{2,1,0:T(2,128)} %all_to_all.107), calls=%async_computation.3 | async-start | bytes 24576 | tf_op jit(solution)/shard_map/all_to_all | solution.py:61
  278.3 4.8 %copy.34 = bf16[2,4,384,768]{3,2,1,0:T(8,128)(2,1)} copy(bf16[2,4,384,768]{3,2,0,1:T(8,128)(2,1)} %bitcast.12) | data formatting | bytes 9437184 | tf_op jit(solution)/shard_map/all_to_all | solution.py:47
  283.1 13.2 %select_reduce_fusion = f32[2,1536]{1,0:T(2,128)S(1)} fusion(bf16[2,1536,768]{2,1,0:T(8,128)(2,1)} %bitcast.32, f32[2,1536]{1,0:T(2,128)S(1)} %bitcast.41, s32[2,1536]{1,0:T(2,128)S(1)} %bitcast.40, s32[2,1536]{1,0:T(2,128)S(1)} %bitcast.39), kind=kOutput, calls=%fused_computation.4 | convolution fusion | flops 7280784384 | bytes 4767744 | tf_op jit(solution)/shard_map/cqd,ckd->cqk/dot_general | solution.py:21
  296.8 19.7 %all_to_all.133 = f32[2,64,4,6]{3,2,0,1:T(4,128)S(1)} all-to-all(f32[2,64,4,6]{3,2,0,1:T(4,128)S(1)} %copy.35), channel_id=1, replica_groups=mesh['gx'=64,'gy'=4] {'gx'}, dimensions={1} | all-to-all | bytes 24576 | tf_op jit(solution)/shard_map/all_to_all | solution.py:83
  316.6 8.0 %all_to_all.134 = f32[128,1,4,6]{0,1,3,2:T(1,128)S(1)} all-to-all(f32[128,1,4,6]{0,1,3,2:T(1,128)S(1)} %copy.37), channel_id=1, replica_groups=mesh['gx'=64,'gy'=4] {'gy'}, dimensions={2} | all-to-all | bytes 24576 | tf_op jit(solution)/shard_map/all_to_all | solution.py:82
  325.2 10.5 %gather_fusion = f32[1024]{0:T(1024)} fusion(f32[3072]{0:T(1024)S(1)} %reshape.62, s32[1024]{0:T(1024)S(1)} %get-tuple-element.5), kind=kCustom, calls=%fused_computation | custom fusion | bytes 12288 | tf_op jit(solution)/shard_map/gather | solution.py:90
  (16 shorter events, 4.2 us)
Async XLA Ops:
  7.4 30.3 %all-to-all-start = ((s32[64,8,6]{2,1,0:T(8,128)}), s32[64,8,6]{2,1,0:T(8,128)S(1)}, u32[]{:S(2)}, u32[]{:S(2)}) async-start(s32[64,8,6]{2,1,0:T(8,128)} %all_to_all.98), calls=%async_computation | async-start | bytes 524288 | tf_op jit(solution)/shard_map/all_to_all | solution.py:55
  37.7 149.0 %all-to-all-start.4 = ((bf16[512,6,768]{2,1,0:T(8,128)(2,1)}), bf16[512,6,768]{2,1,0:T(8,128)(2,1)}, u32[]{:S(2)}, u32[]{:S(2)}) async-start(bf16[512,6,768]{2,1,0:T(8,128)(2,1)} %reshape.60), calls=%async_computation.4 | async-start | bytes 12582912 | tf_op jit(solution)/shard_map/all_to_all | solution.py:48
  186.7 21.5 %all-to-all-start.2 = ((s32[64,8,6]{2,1,0:T(8,128)}), s32[64,8,6]{2,1,0:T(8,128)S(1)}, u32[]{:S(2)}, u32[]{:S(2)}) async-start(s32[64,8,6]{2,1,0:T(8,128)} %all_to_all.104), calls=%async_computation.2 | async-start | bytes 524288 | tf_op jit(solution)/shard_map/all_to_all | solution.py:62
  208.2 59.3 %all-to-all-start.5 = ((bf16[8,384,768]{2,1,0:T(8,128)(2,1)}), bf16[8,384,768]{2,1,0:T(8,128)(2,1)}, u32[]{:S(2)}, u32[]{:S(2)}) async-start(bf16[8,384,768]{2,1,0:T(8,128)(2,1)} %copy.33), calls=%async_computation.5 | async-start | bytes 9437184 | tf_op jit(solution)/shard_map/all_to_all | solution.py:47
  267.5 7.4 %all-to-all-start.1 = ((s32[4,2,384]{2,1,0:T(2,128)}), s32[4,2,384]{2,1,0:T(2,128)S(1)}, u32[]{:S(2)}, u32[]{:S(2)}) async-start(s32[4,2,384]{2,1,0:T(2,128)} %all_to_all.101), calls=%async_computation.1 | async-start | bytes 24576 | tf_op jit(solution)/shard_map/all_to_all | solution.py:54
  274.9 8.2 %all-to-all-start.3 = ((s32[4,2,384]{2,1,0:T(2,128)}), s32[4,2,384]{2,1,0:T(2,128)S(1)}, u32[]{:S(2)}, u32[]{:S(2)}) async-start(s32[4,2,384]{2,1,0:T(2,128)} %all_to_all.107), calls=%async_computation.3 | async-start | bytes 24576 | tf_op jit(solution)/shard_map/all_to_all | solution.py:61
where the time goes:
time: 337 us; the launch traced here: 336 us
  waiting for transfers between devices  193 us (57%)
  local copies, waits for them, and re-layouts  53.4 us (16%)
  starting transfers between devices  43.3 us (13%)
  blocking collectives  27.7 us (8%)
  matrix products  13.2 us (4%)
  other arithmetic  5.34 us (2%)
    all_to_all x1, waiting for transfers between devices, shards(): lax.all_to_all(outgoing, 'gx', split_axis=0, concat_axis=1, tiled=True)  133 us
    all_to_all x1, waiting for transfers between devices, shards(): lax.all_to_all(lax.all_to_all(outgoing, 'gx', split_axis=0, concat_axis=1...  52.7 us
    all_to_all x1, blocking collectives, shards(): lax.all_to_all(arranged, 'gx', split_axis=1, concat_axis=0, tiled=True)  19.7 us
    dot_general x1, matrix products, cluster_max(): jnp.einsum('cqd,ckd->cqk', query_rows, key_rows, preferred_element_type=j...  13.2 us
    all_to_all x1, starting transfers between devices, shards(): lax.all_to_all(out_order, 'gx', split_axis=0, concat_axis=1, tiled=True)  13 us
    gather x1, local copies, waits for them, and re-layouts, shards(): return returned.reshape(-1)[target]  10.5 us
    all_to_all x1, starting transfers between devices, shards(): lax.all_to_all(outgoing, 'gx', split_axis=0, concat_axis=1, tiled=True)  10.5 us
    scatter x1, local copies, waits for them, and re-layouts, shards(): jnp.zeros((cluster_total * slots, width), embeddings.dtype).at[target]  8.81 us
  transfers between devices with their start and end apart: 6, of which 4 were waited for; matrix products, arithmetic and copies ran while one was open for 11% of the time, Pallas kernels for 0%

commit v1 on v0

v1 whole, which is shorter than its diff:
```python
import functools

import jax
import jax.numpy as jnp
from jax import lax
from jax.experimental import pallas as pl
from jax.experimental.pallas import tpu as pltpu
from jax.sharding import PartitionSpec as P

CLUS_DEV = 2
OWN_CAP = 6
LANES = 128
META = 2
DIGIT = 128

norm_eps = 1e-06
bf16 = jnp.bfloat16
f32 = jnp.float32


def iota(shape, dim):
    return lax.broadcasted_iota(jnp.int32, shape, dim)


def pack_kernel(label_span, c_ref, p_ref, x_ref, w_ref, slot_ref, wide_ref):
    owners, rows = slot_ref.shape
    width = x_ref.shape[1]
    parts = width // LANES
    stride = w_ref.shape[0] // owners
    block = min(256, rows)
    clusters = c_ref[...]
    owner = clusters // CLUS_DEV
    key = (clusters % CLUS_DEV) * label_span + p_ref[...] + 1
    before = (iota((block, block), 0) < iota((block, block), 1)).astype(f32).astype(bf16)
    carry = jnp.zeros((owners, 1), f32)
    for b in range(rows // block):
        cols = slice(b * block, (b + 1) * block)
        named = iota((owners, block), 0) == owner[:, cols]
        ones = named.astype(f32)
        rank = jnp.dot(ones.astype(bf16), before, preferred_element_type=f32) + carry
        slot_ref[:, cols] = jnp.where(named, rank, -1.0)
        carry = carry + jnp.sum(ones, axis=1, keepdims=True)
    kind = iota((LANES, rows), 0) % 8
    digits = jnp.where(
        kind == 0,
        key % DIGIT,
        jnp.where(kind == 1, key // DIGIT % DIGIT, jnp.where(kind == 2, key // DIGIT**2, 0)),
    )
    digits = digits.astype(f32).astype(bf16)
    lane = iota((owners, LANES), 1) // 8
    meta = jnp.zeros((owners, LANES), f32)
    for q in range(OWN_CAP):
        pick = (slot_ref[...] == q).astype(f32).astype(bf16)
        picked = jnp.dot(pick, x_ref[...], preferred_element_type=f32)
        for k in range(parts):
            wide_ref[pl.ds(q * parts + k, owners, stride=stride), :] = picked[
                :, k * LANES : (k + 1) * LANES
            ]
        digit = lax.dot_general(
            pick, digits, (((1,), (1,)), ((), ())), preferred_element_type=f32
        )
        meta = jnp.where(lane == q, digit, meta)
    wide_ref[pl.ds(OWN_CAP * parts, owners, stride=stride), :] = meta
    wide_ref[pl.ds(OWN_CAP * parts + 1, owners, stride=stride), :] = jnp.zeros_like(meta)
    w_ref[...] = wide_ref[...].astype(bf16)


def score_kernel(label_span, w_ref, out_ref, wide_ref, x_ref):
    sources = out_ref.shape[0]
    width = x_ref.shape[1]
    parts = width // LANES
    stride = w_ref.shape[0] // sources
    wide_ref[...] = w_ref[...].astype(f32)
    meta = wide_ref[pl.ds(OWN_CAP * parts, sources, stride=stride), :]
    lane = iota((sources, LANES), 1)
    table = jnp.zeros((sources, LANES), f32)
    keys, scales = [], []
    for r in range(OWN_CAP):
        squares = jnp.zeros((sources, LANES), f32)
        for k in range(parts):
            part = wide_ref[pl.ds(r * parts + k, sources, stride=stride), :]
            x_ref[r * sources : (r + 1) * sources, k * LANES : (k + 1) * LANES] = part.astype(bf16)
            squares = squares + part * part
        scale = lax.rsqrt(jnp.sum(squares, axis=1, keepdims=True) + norm_eps)
        key = (
            meta[:, 8 * r : 8 * r + 1]
            + DIGIT * meta[:, 8 * r + 1 : 8 * r + 2]
            + DIGIT**2 * meta[:, 8 * r + 2 : 8 * r + 3]
        )
        keys.append(key)
        scales.append(scale)
        table = jnp.where(lane == r, key, jnp.where(lane == r + 8, scale, table))
    turned = table.T
    result = jnp.full((sources, LANES), -1.0, f32)
    for r in range(OWN_CAP):
        query = x_ref[r * sources : (r + 1) * sources, :]
        low = jnp.where(keys[r] > label_span, float(label_span), 0.0)
        best = jnp.full((sources, sources), -jnp.inf, f32)
        for t in range(OWN_CAP):
            scores = lax.dot_general(
                query,
                x_ref[t * sources : (t + 1) * sources, :],
                (((1,), (1,)), ((), ())),
                preferred_element_type=f32,
            )
            scores = scores * turned[t + 8 : t + 9, :]
            other = turned[t : t + 1, :]
            allowed = (other < keys[r]) & (other > low)
            best = jnp.maximum(best, jnp.where(allowed, scores, -jnp.inf))
        top = jnp.max(best, axis=1, keepdims=True) * scales[r]
        result = jnp.where(lane == r, jnp.maximum(top, -1.0), result)
    out_ref[...] = result[:, :OWN_CAP]


def pick_kernel(r_ref, slot_ref, out_ref):
    slot = slot_ref[...]
    value = jnp.zeros(slot.shape, f32)
    for q in range(OWN_CAP):
        value = jnp.where(slot == q, r_ref[:, q : q + 1], value)
    out_ref[...] = jnp.sum(value, axis=0, keepdims=True)


def call(kernel, out_shape, scratch, name):
    return pl.pallas_call(
        kernel,
        out_shape=out_shape,
        scratch_shapes=scratch,
        compiler_params=pltpu.CompilerParams(vmem_limit_bytes=48 * 2**20),
        name=name,
    )


def shards(embeddings, clusters, priorities):
    rows, width = embeddings.shape
    owners = lax.axis_size("gx") * lax.axis_size("gy")
    label_span = rows * owners
    height = owners * (OWN_CAP * width // LANES + META)
    wide = pltpu.VMEM((height, LANES), f32)
    packed, slot = call(
        functools.partial(pack_kernel, label_span),
        (
            jax.ShapeDtypeStruct((height, LANES), bf16),
            jax.ShapeDtypeStruct((owners, rows), f32),
        ),
        [wide],
        "pack",
    )(clusters.reshape(1, rows), priorities.reshape(1, rows), embeddings)
    arrived = lax.all_to_all(
        packed.reshape(owners, height // owners // 2, 2, LANES),
        ("gx", "gy"),
        split_axis=0,
        concat_axis=0,
        tiled=True,
    ).reshape(height, LANES)
    result = call(
        functools.partial(score_kernel, label_span),
        jax.ShapeDtypeStruct((owners, OWN_CAP), f32),
        [wide, pltpu.VMEM((OWN_CAP * owners, width), bf16)],
        "score",
    )(arrived)
    returned = lax.all_to_all(result, ("gx", "gy"), split_axis=0, concat_axis=0, tiled=True)
    best = call(pick_kernel, jax.ShapeDtypeStruct((1, rows), f32), [], "pick")(returned, slot)
    return best.reshape(rows)


def solution(mesh):
    in_specs = (P(("gx", "gy"), None), P(("gx", "gy")), P(("gx", "gy")))
    out_specs = P(("gx", "gy"))
    return jax.shard_map(shards, mesh=mesh, in_specs=in_specs, out_specs=out_specs, check_vma=False)
```

time: 337 us -> 110 us (0.33)
  waiting for transfers between devices: 193 us -> 0 us
  blocking collectives: 27.7 us -> 96.4 us
  local copies, waits for them, and re-layouts: 53.4 us -> 2.78 us
  starting transfers between devices: 43.3 us -> 0 us
  matrix products: 13.2 us -> 0 us
  Pallas kernels: 0 us -> 10.7 us
  other arithmetic: 5.34 us -> 0 us
    all_to_all x6 -> x0, waiting for transfers between devices: 193 us -> none  [the longest x1 133 us: shards(): lax.all_to_all(outgoing, 'gx', split_axis=0, concat_axis=1, tiled=True)]
    all_to_all x2, blocking collectives: 27.7 us -> 96.4 us  [the longest x1 77 us: shards(): lax.all_to_all(packed.reshape(owners, height // owners // 2, 2, LANES), (...]
    all_to_all x6 -> x0, starting transfers between devices: 43.3 us -> none  [the longest x1 13 us: shards(): lax.all_to_all(out_order, 'gx', split_axis=0, concat_axis=1, tiled=True)]
    scatter x3 -> x0, local copies, waits for them, and re-layouts: 17.8 us -> none  [the longest x1 8.81 us: shards(): jnp.zeros((cluster_total * slots, width), embeddings.dtype).at[target]]
    all_to_all x11 -> x0, local copies, waits for them, and re-layouts: 15.8 us -> none  [the longest x2 7.23 us: shards(): lax.all_to_all(outgoing, 'gx', split_axis=0, concat_axis=1, tiled=True)]
    dot_general x1 -> x0, matrix products: 13.2 us -> none  [cluster_max(): jnp.einsum('cqd,ckd->cqk', query_rows, key_rows, preferred_element_type=j...]
    pallas_call x0 -> x3, Pallas kernels: none -> 10.7 us  [the longest x1 5.32 us: shards(): call(functools.partial(score_kernel, label_span), jax.ShapeDtypeStruct((o...]
    gather x1 -> x0, local copies, waits for them, and re-layouts: 10.5 us -> none  [shards(): return returned.reshape(-1)[target]]
  transfers between devices with their start and end apart: 6 -> 0, of which waited for: 4 -> 0; matrix products, arithmetic and copies ran while one was open for 11% -> 0% of each run, Pallas kernels for 0% -> 0%
where the time goes in v1:
time: 110 us
  blocking collectives  96.4 us (88%)
  Pallas kernels  10.7 us (10%)
  local copies, waits for them, and re-layouts  2.78 us (3%)
    all_to_all x1, blocking collectives, shards(): lax.all_to_all(packed.reshape(owners, height // owners // 2, 2, LANES), (...  77 us
    all_to_all x1, blocking collectives, shards(): lax.all_to_all(result, ('gx', 'gy'), split_axis=0, concat_axis=0, tiled=T...  19.4 us
    pallas_call x1, Pallas kernels, shards(): call(functools.partial(score_kernel, label_span), jax.ShapeDtypeStruct((o...  5.32 us
    pallas_call x1, Pallas kernels, shards(): call(functools.partial(pack_kernel, label_span), (jax.ShapeDtypeStruct((h...  4.15 us
    unnamed x6, local copies, waits for them, and re-layouts  2.78 us

profile of v1, /device:TPU:1, one launch (start us, length us, event | category | flops | bytes accessed | tf_op | source)
XLA Modules:
  0.0 109.9 jit_solution(13195962877673173782)
XLA Ops:
  0.0 0.0 copy-start
  0.0 1.4 %copy-done = bf16[1024,768]{1,0:T(8,128)(2,1)S(1)} copy-done((bf16[1024,768]{1,0:T(8,128)(2,1)S(1)}, bf16[1024,768]{1,0:T(8,128)(2,1)}, u32[]{:S(2)}) %copy-start) | copy-done | bytes 1572888
  1.4 0.0 copy-start.1
  1.4 0.7 copy-done.1
  2.1 0.0 copy-start.2
  2.1 0.7 copy-done.2
  2.8 4.2 %pack.1 = (bf16[9728,128]{1,0:T(8,128)(2,1)S(1)}, f32[256,1024]{1,0:T(8,128)S(1)}) custom-call(s32[1,1024]{1,0:T(1,128)S(1)} %bitcast.13, s32[1,1024]{1,0:T(1,128)S(1)} %bitcast.14, bf16[1024,768]{1,0:T(8,128)(2,1)S(1)} %copy-done), custom_call_target="tpu_custom_call" | custom-call | tf_op jit(solution)/shard_map/pack/pallas_call | solution.py:139
  6.9 77.0 %all_to_all.16 = bf16[256,19,2,128]{3,2,1,0:T(2,128)(2,1)S(1)} all-to-all(bf16[256,19,2,128]{3,2,1,0:T(2,128)(2,1)S(1)} %bitcast.10), channel_id=1, replica_groups=mesh['gx'=64,'gy'=4] {'gx','gy'}, dimensions={0} | all-to-all | bytes 4980736 | tf_op jit(solution)/shard_map/all_to_all | solution.py:148
  84.0 5.3 %score.1 = f32[256,6]{1,0:T(8,128)S(1)} custom-call(bf16[9728,128]{1,0:T(8,128)(2,1)S(1)} %bitcast.9), custom_call_target="tpu_custom_call" | custom-call | tf_op jit(solution)/shard_map/score/pallas_call | solution.py:155
  89.3 19.4 %all_to_all.17 = f32[256,1,6]{2,1,0:T(1,128)S(1)} all-to-all(f32[256,1,6]{2,1,0:T(1,128)S(1)} %bitcast.12), channel_id=1, replica_groups=mesh['gx'=64,'gy'=4] {'gx','gy'}, dimensions={0} | all-to-all | bytes 12288 | tf_op jit(solution)/shard_map/all_to_all | solution.py:161
  108.7 1.3 %pick.1 = f32[1,1024]{1,0:T(1,128)} custom-call(f32[256,6]{1,0:T(8,128)S(1)} %bitcast.11, f32[256,1024]{1,0:T(8,128)S(1)} %get-tuple-element.8.slot_ref), custom_call_target="tpu_custom_call" | custom-call | tf_op jit(solution)/shard_map/pick/pallas_call | solution.py:162
Async XLA Ops:
  0.0 1.4 %copy-start = (bf16[1024,768]{1,0:T(8,128)(2,1)S(1)}, bf16[1024,768]{1,0:T(8,128)(2,1)}, u32[]{:S(2)}) copy-start(bf16[1024,768]{1,0:T(8,128)(2,1)} %x_ref.1) | copy-start | bytes 4718596
  1.4 0.7 copy-start.1
  2.1 0.7 copy-start.2

commit v2 on v1

v2 whole, which is shorter than its diff:
```python
import functools

import jax
import jax.numpy as jnp
from jax import lax
from jax.experimental import pallas as pl
from jax.experimental.pallas import tpu as pltpu
from jax.sharding import PartitionSpec as P

CLUS_DEV = 2
OWN_CAP = 6
LANES = 128
META = 2
DIGIT = 128
X_PIECES = 1
STEP = 32

norm_eps = 1e-06
bf16 = jnp.bfloat16
f32 = jnp.float32


def iota(shape, dim):
    return lax.broadcasted_iota(jnp.int32, shape, dim)


def pack_kernel(
    label_span, c_hbm, p_hbm, x_hbm, w_ref, slot_ref, wide_ref, c_ref, p_ref, x_ref, sems
):
    owners, rows = slot_ref.shape
    width = x_ref.shape[1]
    parts = width // LANES
    stride = w_ref.shape[0] // owners
    block = min(256, rows)
    copies = [
        pltpu.make_async_copy(c_hbm, c_ref, sems.at[0]),
        pltpu.make_async_copy(p_hbm, p_ref, sems.at[1]),
    ]
    piece = rows // X_PIECES
    for i in range(X_PIECES):
        span = pl.ds(i * piece, piece)
        copies.append(pltpu.make_async_copy(x_hbm.at[span], x_ref.at[span], sems.at[2 + i]))
    for copy in copies:
        copy.start()
    before = (iota((block, block), 0) < iota((block, block), 1)).astype(f32).astype(bf16)
    copies[0].wait()
    copies[1].wait()
    clusters = c_ref[...]
    owner = clusters // CLUS_DEV
    key = (clusters % CLUS_DEV) * label_span + p_ref[...] + 1
    ones = jnp.ones((block, block), bf16)
    earlier = None
    for b in range(rows // block):
        cols = slice(b * block, (b + 1) * block)
        named = iota((owners, block), 0) == owner[:, cols]
        count = named.astype(f32).astype(bf16)
        rank = jnp.dot(count, before, preferred_element_type=f32)
        if b:
            rank = rank + jnp.dot(earlier, ones, preferred_element_type=f32)
        earlier = earlier + count if b else count
        slot_ref[:, cols] = jnp.where(named, rank, -1.0)
    key = key.astype(f32)
    lane = iota((owners, LANES), 1)
    table = jnp.zeros((owners, LANES), f32)
    for copy in copies[2:]:
        copy.wait()
    for q in range(OWN_CAP):
        hit = slot_ref[...] == q
        pick = jnp.where(hit, 1.0, 0.0).astype(bf16)
        picked = jnp.dot(pick, x_ref[...], preferred_element_type=f32)
        for k in range(parts):
            wide_ref[pl.ds(q * parts + k, owners, stride=stride), :] = picked[
                :, k * LANES : (k + 1) * LANES
            ]
        held = jnp.sum(jnp.where(hit, key, 0.0), axis=1, keepdims=True)
        table = jnp.where(lane // 8 == q, held, table)
    table = table.astype(jnp.int32)
    meta = jnp.where(
        lane % 8 == 0,
        table % DIGIT,
        jnp.where(
            lane % 8 == 1,
            table // DIGIT % DIGIT,
            jnp.where(lane % 8 == 2, table // DIGIT**2, 0),
        ),
    ).astype(f32)
    wide_ref[pl.ds(OWN_CAP * parts, owners, stride=stride), :] = meta
    wide_ref[pl.ds(OWN_CAP * parts + 1, owners, stride=stride), :] = jnp.zeros_like(meta)
    w_ref[...] = wide_ref[...].astype(bf16)


def score_kernel(
    label_span, w_ref, out_ref, wide_ref, x_ref, key_ref, label_ref, scale_ref, turned_ref
):
    sources = out_ref.shape[0]
    width = x_ref.shape[1]
    parts = width // LANES
    stride = w_ref.shape[0] // sources
    minus = -jnp.inf
    wide_ref[...] = w_ref[...].astype(f32)
    meta = wide_ref[pl.ds(OWN_CAP * parts, sources, stride=stride), :]
    lane = iota((sources, LANES), 1)
    table = jnp.zeros((sources, LANES), f32)
    for r in range(OWN_CAP):
        own = slice(r * sources, (r + 1) * sources)
        key = (
            meta[:, 8 * r : 8 * r + 1]
            + DIGIT * meta[:, 8 * r + 1 : 8 * r + 2]
            + DIGIT**2 * meta[:, 8 * r + 2 : 8 * r + 3]
        )
        label = jnp.where(key > label_span, 1.0, jnp.where(key > 0, 0.0, 2.0))
        key_ref[own, :] = jnp.broadcast_to(key, (sources, LANES))
        label_ref[own, :] = jnp.broadcast_to(label, (sources, LANES))
        table = jnp.where(lane == r, key, jnp.where(lane == r + 8, label, table))
    turned_ref[...] = table.T
    here = iota((sources, sources), 0) == iota((sources, sources), 1)
    result = jnp.full((sources, LANES), -1.0, f32)
    tops = jnp.full((8, sources), -1.0, f32)
    halves = sources // LANES
    second = [[jnp.full((8, LANES), minus, f32)] * halves for _ in range(OWN_CAP)]
    for r in range(OWN_CAP):
        own = slice(r * sources, (r + 1) * sources)
        for k in range(parts):
            x_ref[own, k * LANES : (k + 1) * LANES] = wide_ref[
                pl.ds(r * parts + k, sources, stride=stride), :
            ].astype(bf16)
        first = [jnp.full((STEP, LANES), minus, f32)] * (sources // STEP)
        for t in [r, *range(r)]:
            scores = lax.dot_general(
                x_ref[own, :],
                x_ref[t * sources : (t + 1) * sources, :],
                (((1,), (1,)), ((), ())),
                preferred_element_type=f32,
            )
            if t == r:
                squares = jnp.where(here, scores, 0.0)
                scale = lax.rsqrt(jnp.sum(squares, axis=1, keepdims=True) + norm_eps)
                scale_ref[own, :] = jnp.broadcast_to(scale, (sources, LANES))
                turned_ref[16 + r : 17 + r, :] = lax.rsqrt(
                    jnp.sum(squares, axis=0, keepdims=True) + norm_eps
                )
            for i in range(sources // STEP):
                rows = slice(i * STEP, (i + 1) * STEP)
                at = slice(r * sources + i * STEP, r * sources + (i + 1) * STEP)
                for h in range(halves):
                    cols = slice(h * LANES, (h + 1) * LANES)
                    like = label_ref[at, :] == turned_ref[8 + t : 9 + t, cols]
                    score = jnp.where(like, scores[rows, cols], minus)
                    later = turned_ref[t : t + 1, cols] < key_ref[at, :]
                    forward = jnp.where(later, score * turned_ref[16 + t : 17 + t, cols], minus)
                    first[i] = jnp.maximum(first[i], forward)
                    if t != r:
                        back = jnp.where(later, minus, score * scale_ref[at, :])
                        back = jnp.max(back.reshape(STEP // 8, 8, LANES), axis=0)
                        second[t][h] = jnp.maximum(second[t][h], back)
        top = jnp.concatenate([jnp.max(f, axis=1, keepdims=True) for f in first], axis=0)
        result = jnp.where(lane == r, top * scale_ref[own, :], result)
    for t in range(OWN_CAP):
        top = jnp.concatenate([jnp.max(s, axis=0, keepdims=True) for s in second[t]], axis=1)
        top = top * turned_ref[16 + t : 17 + t, :]
        tops = jnp.where(iota((8, sources), 0) == t, top, tops)
    turned_ref[:8, :] = tops
    result = jnp.maximum(jnp.maximum(result, turned_ref[...].T), -1.0)
    out_ref[...] = result[:, :OWN_CAP]


def pick_kernel(r_ref, slot_ref, out_ref):
    slot = slot_ref[...]
    value = jnp.zeros(slot.shape, f32)
    for q in range(OWN_CAP):
        value = jnp.where(slot == q, r_ref[:, q : q + 1], value)
    out_ref[...] = jnp.sum(value, axis=0, keepdims=True)


def call(kernel, out_shape, scratch, name, **rest):
    return pl.pallas_call(
        kernel,
        out_shape=out_shape,
        scratch_shapes=scratch,
        compiler_params=pltpu.CompilerParams(vmem_limit_bytes=48 * 2**20),
        name=name,
        **rest,
    )


def stay(value):
    return pltpu.with_memory_space_constraint(value, pltpu.HBM)


def shards(embeddings, clusters, priorities):
    rows, width = embeddings.shape
    owners = lax.axis_size("gx") * lax.axis_size("gy")
    label_span = rows * owners
    height = owners * (OWN_CAP * width // LANES + META)
    slots = owners * OWN_CAP
    wide = pltpu.VMEM((height, LANES), f32)
    packed, slot = call(
        functools.partial(pack_kernel, label_span),
        (
            jax.ShapeDtypeStruct((height, LANES), bf16),
            jax.ShapeDtypeStruct((owners, rows), f32),
        ),
        [
            wide,
            pltpu.VMEM((1, rows), jnp.int32),
            pltpu.VMEM((1, rows), jnp.int32),
            pltpu.VMEM((rows, width), bf16),
            pltpu.SemaphoreType.DMA((2 + X_PIECES,)),
        ],
        "pack",
        in_specs=[pl.BlockSpec(memory_space=pltpu.HBM)] * 3,
    )(stay(clusters.reshape(1, rows)), stay(priorities.reshape(1, rows)), stay(embeddings))
    arrived = lax.all_to_all(
        packed.reshape(owners, height // owners // 2, 2, LANES),
        ("gx", "gy"),
        split_axis=0,
        concat_axis=0,
        tiled=True,
    ).reshape(height, LANES)
    result = call(
        functools.partial(score_kernel, label_span),
        jax.ShapeDtypeStruct((owners, OWN_CAP), f32),
        [
            wide,
            pltpu.VMEM((slots, width), bf16),
            pltpu.VMEM((slots, LANES), f32),
            pltpu.VMEM((slots, LANES), f32),
            pltpu.VMEM((slots, LANES), f32),
            pltpu.VMEM((LANES, owners), f32),
        ],
        "score",
    )(arrived)
    returned = lax.all_to_all(result, ("gx", "gy"), split_axis=0, concat_axis=0, tiled=True)
    best = call(pick_kernel, jax.ShapeDtypeStruct((1, rows), f32), [], "pick")(returned, slot)
    return best.reshape(rows)


def solution(mesh):
    in_specs = (P(("gx", "gy"), None), P(("gx", "gy")), P(("gx", "gy")))
    out_specs = P(("gx", "gy"))
    return jax.shard_map(shards, mesh=mesh, in_specs=in_specs, out_specs=out_specs, check_vma=False)
```

time: 110 us -> 107 us (0.973)
  local copies, waits for them, and re-layouts: 2.78 us -> 0 us
    unnamed x6 -> x0, local copies, waits for them, and re-layouts: 2.78 us -> none
where the time goes in v2:
time: 107 us
  blocking collectives  96.4 us (90%)
  Pallas kernels  10.5 us (10%)
    all_to_all x1, blocking collectives, shards(): lax.all_to_all(packed.reshape(owners, height // owners // 2, 2, LANES), (...  77 us
    all_to_all x1, blocking collectives, shards(): lax.all_to_all(result, ('gx', 'gy'), split_axis=0, concat_axis=0, tiled=T...  19.3 us
    pallas_call x1, Pallas kernels, shards(): call(functools.partial(pack_kernel, label_span), (jax.ShapeDtypeStruct((h...  4.87 us
    pallas_call x1, Pallas kernels, shards(): call(functools.partial(score_kernel, label_span), jax.ShapeDtypeStruct((o...  4.36 us

profile of v2, /device:TPU:1, one launch (start us, length us, event | category | flops | bytes accessed | tf_op | source)
XLA Modules:
  0.0 106.9 jit_solution(2685292573991144877)
XLA Ops:
  0.0 4.9 %pack.1 = (bf16[9728,128]{1,0:T(8,128)(2,1)S(1)}, f32[256,1024]{1,0:T(8,128)S(1)}) custom-call(s32[1,1024]{1,0:T(1,128)} %bitcast.13, s32[1,1024]{1,0:T(1,128)} %bitcast.14, bf16[1024,768]{1,0:T(8,128)(2,1)} %x_hbm.1), custom_call_target="tpu_custom_call" | custom-call | tf_op jit(solution)/shard_map/pack/pallas_call | solution.py:197
  4.9 77.0 %all_to_all.16 = bf16[256,19,2,128]{3,2,1,0:T(2,128)(2,1)S(1)} all-to-all(bf16[256,19,2,128]{3,2,1,0:T(2,128)(2,1)S(1)} %bitcast.10), channel_id=1, replica_groups=mesh['gx'=64,'gy'=4] {'gx','gy'}, dimensions={0} | all-to-all | bytes 4980736 | tf_op jit(solution)/shard_map/all_to_all | solution.py:213
  81.9 4.4 %score.1 = f32[256,6]{1,0:T(8,128)S(1)} custom-call(bf16[9728,128]{1,0:T(8,128)(2,1)S(1)} %bitcast.9), custom_call_target="tpu_custom_call" | custom-call | tf_op jit(solution)/shard_map/score/pallas_call | solution.py:220
  86.3 19.3 %all_to_all.17 = f32[256,1,6]{2,1,0:T(1,128)S(1)} all-to-all(f32[256,1,6]{2,1,0:T(1,128)S(1)} %bitcast.12), channel_id=1, replica_groups=mesh['gx'=64,'gy'=4] {'gx','gy'}, dimensions={0} | all-to-all | bytes 12288 | tf_op jit(solution)/shard_map/all_to_all | solution.py:233
  105.6 1.3 %pick.1 = f32[1,1024]{1,0:T(1,128)} custom-call(f32[256,6]{1,0:T(8,128)S(1)} %bitcast.11, f32[256,1024]{1,0:T(8,128)S(1)} %get-tuple-element.8.slot_ref), custom_call_target="tpu_custom_call" | custom-call | tf_op jit(solution)/shard_map/pick/pallas_call | solution.py:234

commit v3 on v2

--- a/solution.py
+++ b/solution.py
@@ -13,7 +13,7 @@
 META = 2
 DIGIT = 128
 X_PIECES = 1
-STEP = 32
+WIDE = 256
 
 norm_eps = 1e-06
 bf16 = jnp.bfloat16
@@ -25,7 +25,7 @@
 
 
 def pack_kernel(
-    label_span, c_hbm, p_hbm, x_hbm, w_ref, slot_ref, wide_ref, c_ref, p_ref, x_ref, sems
+    label_span, c_hbm, p_hbm, x_hbm, w_ref, slot_ref, wide_ref, c_ref, p_ref, x_ref, sems, pick_ref
 ):
     owners, rows = slot_ref.shape
     width = x_ref.shape[1]
@@ -62,18 +62,23 @@
     key = key.astype(f32)
     lane = iota((owners, LANES), 1)
     table = jnp.zeros((owners, LANES), f32)
+    for q in range(OWN_CAP):
+        hit = slot_ref[...] == q
+        pick_ref[q * owners : (q + 1) * owners, :] = jnp.where(hit, 1.0, 0.0).astype(bf16)
+        held = jnp.sum(jnp.where(hit, key, 0.0), axis=1, keepdims=True)
+        table = jnp.where(lane // 8 == q, held, table)
     for copy in copies[2:]:
         copy.wait()
-    for q in range(OWN_CAP):
-        hit = slot_ref[...] == q
-        pick = jnp.where(hit, 1.0, 0.0).astype(bf16)
-        picked = jnp.dot(pick, x_ref[...], preferred_element_type=f32)
-        for k in range(parts):
-            wide_ref[pl.ds(q * parts + k, owners, stride=stride), :] = picked[
-                :, k * LANES : (k + 1) * LANES
-            ]
-        held = jnp.sum(jnp.where(hit, key, 0.0), axis=1, keepdims=True)
-        table = jnp.where(lane // 8 == q, held, table)
+    for n in range(width // WIDE):
+        picked = jnp.dot(
+            pick_ref[...], x_ref[:, n * WIDE : (n + 1) * WIDE], preferred_element_type=f32
+        )
+        for q in range(OWN_CAP):
+            for h in range(WIDE // LANES):
+                at = q * parts + n * (WIDE // LANES) + h
+                wide_ref[pl.ds(at, owners, stride=stride), :] = picked[
+                    q * owners : (q + 1) * owners, h * LANES : (h + 1) * LANES
+                ]
     table = table.astype(jnp.int32)
     meta = jnp.where(
         lane % 8 == 0,
@@ -90,7 +95,7 @@
 
 
 def score_kernel(
-    label_span, w_ref, out_ref, wide_ref, x_ref, key_ref, label_ref, scale_ref, turned_ref
+    label_span, w_ref, out_ref, wide_ref, x_ref, key_ref, label_ref, scale_ref, turned_ref, tile_ref, first_ref
 ):
     sources = out_ref.shape[0]
     width = x_ref.shape[1]
@@ -118,43 +123,52 @@
     tops = jnp.full((8, sources), -1.0, f32)
     halves = sources // LANES
     second = [[jnp.full((8, LANES), minus, f32)] * halves for _ in range(OWN_CAP)]
-    for r in range(OWN_CAP):
+    first = {}
+    tiles = [(r, t) for r in range(OWN_CAP) for t in [r, *range(r)]]
+    for m, (r, t) in enumerate(tiles):
         own = slice(r * sources, (r + 1) * sources)
-        for k in range(parts):
-            x_ref[own, k * LANES : (k + 1) * LANES] = wide_ref[
-                pl.ds(r * parts + k, sources, stride=stride), :
-            ].astype(bf16)
-        first = [jnp.full((STEP, LANES), minus, f32)] * (sources // STEP)
-        for t in [r, *range(r)]:
-            scores = lax.dot_general(
-                x_ref[own, :],
-                x_ref[t * sources : (t + 1) * sources, :],
-                (((1,), (1,)), ((), ())),
-                preferred_element_type=f32,
+        if t == r:
+            for k in range(parts):
+                x_ref[own, k * LANES : (k + 1) * LANES] = wide_ref[
+                    pl.ds(r * parts + k, sources, stride=stride), :
+                ].astype(bf16)
+        tile_ref[m] = lax.dot_general(
+            x_ref[own, :],
+            x_ref[t * sources : (t + 1) * sources, :],
+            (((1,), (1,)), ((), ())),
+            preferred_element_type=f32,
+        )
+        if t == r:
+            squares = jnp.where(here, tile_ref[m], 0.0)
+            scale = lax.rsqrt(jnp.sum(squares, axis=1, keepdims=True) + norm_eps)
+            scale_ref[own, :] = jnp.broadcast_to(scale, (sources, LANES))
+            turned_ref[16 + r : 17 + r, :] = lax.rsqrt(
+                jnp.sum(squares, axis=0, keepdims=True) + norm_eps
             )
-            if t == r:
-                squares = jnp.where(here, scores, 0.0)
-                scale = lax.rsqrt(jnp.sum(squares, axis=1, keepdims=True) + norm_eps)
-                scale_ref[own, :] = jnp.broadcast_to(scale, (sources, LANES))
-                turned_ref[16 + r : 17 + r, :] = lax.rsqrt(
-                    jnp.sum(squares, axis=0, keepdims=True) + norm_eps
-                )
-            for i in range(sources // STEP):
-                rows = slice(i * STEP, (i + 1) * STEP)
-                at = slice(r * sources + i * STEP, r * sources + (i + 1) * STEP)
-                for h in range(halves):
-                    cols = slice(h * LANES, (h + 1) * LANES)
-                    like = label_ref[at, :] == turned_ref[8 + t : 9 + t, cols]
-                    score = jnp.where(like, scores[rows, cols], minus)
-                    later = turned_ref[t : t + 1, cols] < key_ref[at, :]
-                    forward = jnp.where(later, score * turned_ref[16 + t : 17 + t, cols], minus)
-                    first[i] = jnp.maximum(first[i], forward)
-                    if t != r:
-                        back = jnp.where(later, minus, score * scale_ref[at, :])
-                        back = jnp.max(back.reshape(STEP // 8, 8, LANES), axis=0)
-                        second[t][h] = jnp.maximum(second[t][h], back)
-        top = jnp.concatenate([jnp.max(f, axis=1, keepdims=True) for f in first], axis=0)
-        result = jnp.where(lane == r, top * scale_ref[own, :], result)
+        spans = [slice(h * LANES, (h + 1) * LANES) for h in range(halves)]
+        label_row = [jnp.broadcast_to(turned_ref[8 + t : 9 + t, c], (8, LANES)) for c in spans]
+        key_row = [jnp.broadcast_to(turned_ref[t : t + 1, c], (8, LANES)) for c in spans]
+        scale_row = [jnp.broadcast_to(turned_ref[16 + t : 17 + t, c], (8, LANES)) for c in spans]
+        for i in range(sources // 8):
+            at = slice(r * sources + i * 8, r * sources + i * 8 + 8)
+            label_col, key_col = label_ref[at, :], key_ref[at, :]
+            if t != r:
+                scale_col = scale_ref[at, :]
+            forwards = []
+            for h in range(halves):
+                score = tile_ref[m, i * 8 : (i + 1) * 8, spans[h]]
+                score = jnp.where(label_col == label_row[h], score, minus)
+                later = key_row[h] < key_col
+                forward = jnp.where(later, score * scale_row[h], minus)
+                forwards.append(forward)
+                if t != r:
+                    back = jnp.where(later, minus, score * scale_col)
+                    second[t][h] = jnp.maximum(second[t][h], back)
+            best = jnp.maximum(*forwards)
+            first_ref[i * 8 : i * 8 + 8, :] = best if t == r else jnp.maximum(first_ref[i * 8 : i * 8 + 8, :], best)
+        if m + 1 == len(tiles) or tiles[m + 1][0] != r:
+            top = jnp.max(first_ref[...], axis=1, keepdims=True)
+            result = jnp.where(lane == r, top * scale_ref[own, :], result)
     for t in range(OWN_CAP):
         top = jnp.concatenate([jnp.max(s, axis=0, keepdims=True) for s in second[t]], axis=1)
         top = top * turned_ref[16 + t : 17 + t, :]
@@ -206,6 +220,7 @@
             pltpu.VMEM((1, rows), jnp.int32),
             pltpu.VMEM((rows, width), bf16),
             pltpu.SemaphoreType.DMA((2 + X_PIECES,)),
+            pltpu.VMEM((slots, rows), bf16),
         ],
         "pack",
         in_specs=[pl.BlockSpec(memory_space=pltpu.HBM)] * 3,
@@ -227,6 +242,8 @@
             pltpu.VMEM((slots, LANES), f32),
             pltpu.VMEM((slots, LANES), f32),
             pltpu.VMEM((LANES, owners), f32),
+            pltpu.VMEM((OWN_CAP * (OWN_CAP + 1) // 2, owners, owners), f32),
+            pltpu.VMEM((owners, LANES), f32),
         ],
         "score",
     )(arrived)

time: 107 us -> 106 us (level)
  no operation moved by 1% of the time
where the time goes in v3:
time: 106 us
  blocking collectives  96.4 us (91%)
  Pallas kernels  9.91 us (9%)
    all_to_all x1, blocking collectives, shards(): lax.all_to_all(packed.reshape(owners, height // owners // 2, 2, LANES), (...  77 us
    all_to_all x1, blocking collectives, shards(): lax.all_to_all(result, ('gx', 'gy'), split_axis=0, concat_axis=0, tiled=T...  19.3 us
    pallas_call x1, Pallas kernels, shards(): call(functools.partial(pack_kernel, label_span), (jax.ShapeDtypeStruct((h...  4.73 us
    pallas_call x1, Pallas kernels, shards(): call(functools.partial(score_kernel, label_span), jax.ShapeDtypeStruct((o...  3.92 us

profile of v3, /device:TPU:1, one launch (start us, length us, event | category | flops | bytes accessed | tf_op | source)
XLA Modules:
  0.0 106.3 jit_solution(15090371715519005385)
XLA Ops:
  0.0 4.7 %pack.1 = (bf16[9728,128]{1,0:T(8,128)(2,1)S(1)}, f32[256,1024]{1,0:T(8,128)S(1)}) custom-call(s32[1,1024]{1,0:T(1,128)} %bitcast.13, s32[1,1024]{1,0:T(1,128)} %bitcast.14, bf16[1024,768]{1,0:T(8,128)(2,1)} %x_hbm.1), custom_call_target="tpu_custom_call" | custom-call | tf_op jit(solution)/shard_map/pack/pallas_call | solution.py:211
  4.7 77.0 %all_to_all.16 = bf16[256,19,2,128]{3,2,1,0:T(2,128)(2,1)S(1)} all-to-all(bf16[256,19,2,128]{3,2,1,0:T(2,128)(2,1)S(1)} %bitcast.10), channel_id=1, replica_groups=mesh['gx'=64,'gy'=4] {'gx','gy'}, dimensions={0} | all-to-all | bytes 4980736 | tf_op jit(solution)/shard_map/all_to_all | solution.py:228
  81.8 3.9 %score.1 = f32[256,6]{1,0:T(8,128)S(1)} custom-call(bf16[9728,128]{1,0:T(8,128)(2,1)S(1)} %bitcast.9), custom_call_target="tpu_custom_call" | custom-call | tf_op jit(solution)/shard_map/score/pallas_call | solution.py:235
  85.7 19.3 %all_to_all.17 = f32[256,1,6]{2,1,0:T(1,128)S(1)} all-to-all(f32[256,1,6]{2,1,0:T(1,128)S(1)} %bitcast.12), channel_id=1, replica_groups=mesh['gx'=64,'gy'=4] {'gx','gy'}, dimensions={0} | all-to-all | bytes 12288 | tf_op jit(solution)/shard_map/all_to_all | solution.py:250
  105.0 1.3 %pick.1 = f32[1,1024]{1,0:T(1,128)} custom-call(f32[256,6]{1,0:T(8,128)S(1)} %bitcast.11, f32[256,1024]{1,0:T(8,128)S(1)} %get-tuple-element.8.slot_ref), custom_call_target="tpu_custom_call" | custom-call | tf_op jit(solution)/shard_map/pick/pallas_call | solution.py:251

commit v4 on v3

--- a/solution.py
+++ b/solution.py
@@ -13,7 +13,7 @@
 META = 2
 DIGIT = 128
 X_PIECES = 1
-WIDE = 256
+GROUPS = 2
 
 norm_eps = 1e-06
 bf16 = jnp.bfloat16
@@ -25,7 +25,20 @@
 
 
 def pack_kernel(
-    label_span, c_hbm, p_hbm, x_hbm, w_ref, slot_ref, wide_ref, c_ref, p_ref, x_ref, sems, pick_ref
+    label_span,
+    c_hbm,
+    p_hbm,
+    x_hbm,
+    w_ref,
+    named_ref,
+    rank_ref,
+    wide_ref,
+    c_ref,
+    p_ref,
+    x_ref,
+    sems,
+    pick_ref,
+    slot_ref,
 ):
     owners, rows = slot_ref.shape
     width = x_ref.shape[1]
@@ -59,43 +72,61 @@
             rank = rank + jnp.dot(earlier, ones, preferred_element_type=f32)
         earlier = earlier + count if b else count
         slot_ref[:, cols] = jnp.where(named, rank, -1.0)
+        named_ref[:, cols] = count
+        rank_ref[:, cols] = jnp.sum(jnp.where(named, rank, 0.0), axis=0, keepdims=True).astype(jnp.int32)
     key = key.astype(f32)
     lane = iota((owners, LANES), 1)
-    table = jnp.zeros((owners, LANES), f32)
-    for q in range(OWN_CAP):
-        hit = slot_ref[...] == q
-        pick_ref[q * owners : (q + 1) * owners, :] = jnp.where(hit, 1.0, 0.0).astype(bf16)
-        held = jnp.sum(jnp.where(hit, key, 0.0), axis=1, keepdims=True)
-        table = jnp.where(lane // 8 == q, held, table)
     for copy in copies[2:]:
         copy.wait()
-    for n in range(width // WIDE):
+    group = owners // GROUPS
+    for g in range(GROUPS):
+        some = slice(g * group, (g + 1) * group)
+        for q in range(OWN_CAP):
+            hit = slot_ref[some, :] == q
+            at = (g * OWN_CAP + q) * group
+            pick_ref[at : at + group, :] = jnp.where(hit, 1.0, 0.0).astype(bf16)
+            held = jnp.sum(jnp.where(hit, key, 0.0), axis=1, keepdims=True)
+            table_g = jnp.where(lane[some] // 8 == q, held, 0.0 if q == 0 else table_g)
         picked = jnp.dot(
-            pick_ref[...], x_ref[:, n * WIDE : (n + 1) * WIDE], preferred_element_type=f32
+            pick_ref[g * OWN_CAP * group : (g + 1) * OWN_CAP * group, :],
+            x_ref[...],
+            preferred_element_type=f32,
         )
         for q in range(OWN_CAP):
-            for h in range(WIDE // LANES):
-                at = q * parts + n * (WIDE // LANES) + h
-                wide_ref[pl.ds(at, owners, stride=stride), :] = picked[
-                    q * owners : (q + 1) * owners, h * LANES : (h + 1) * LANES
+            for k in range(parts):
+                wide_ref[pl.ds(g * group * stride + q * parts + k, group, stride=stride), :] = picked[
+                    q * group : (q + 1) * group, k * LANES : (k + 1) * LANES
                 ]
-    table = table.astype(jnp.int32)
-    meta = jnp.where(
-        lane % 8 == 0,
-        table % DIGIT,
-        jnp.where(
-            lane % 8 == 1,
-            table // DIGIT % DIGIT,
-            jnp.where(lane % 8 == 2, table // DIGIT**2, 0),
-        ),
-    ).astype(f32)
-    wide_ref[pl.ds(OWN_CAP * parts, owners, stride=stride), :] = meta
-    wide_ref[pl.ds(OWN_CAP * parts + 1, owners, stride=stride), :] = jnp.zeros_like(meta)
-    w_ref[...] = wide_ref[...].astype(bf16)
+        table_g = table_g.astype(jnp.int32)
+        kind = lane[some] % 8
+        meta = jnp.where(
+            kind == 0,
+            table_g % DIGIT,
+            jnp.where(
+                kind == 1,
+                table_g // DIGIT % DIGIT,
+                jnp.where(kind == 2, table_g // DIGIT**2, 0),
+            ),
+        ).astype(f32)
+        at = g * group * stride + OWN_CAP * parts
+        wide_ref[pl.ds(at, group, stride=stride), :] = meta
+        wide_ref[pl.ds(at + 1, group, stride=stride), :] = jnp.zeros_like(meta)
+        whole = slice(g * group * stride, (g + 1) * group * stride)
+        w_ref[whole, :] = wide_ref[whole, :].astype(bf16)
 
 
 def score_kernel(
-    label_span, w_ref, out_ref, wide_ref, x_ref, key_ref, label_ref, scale_ref, turned_ref, tile_ref, first_ref
+    label_span,
+    w_ref,
+    out_ref,
+    wide_ref,
+    x_ref,
+    key_ref,
+    label_ref,
+    scale_ref,
+    turned_ref,
+    tile_ref,
+    first_ref,
 ):
     sources = out_ref.shape[0]
     width = x_ref.shape[1]
@@ -165,7 +196,8 @@
                     back = jnp.where(later, minus, score * scale_col)
                     second[t][h] = jnp.maximum(second[t][h], back)
             best = jnp.maximum(*forwards)
-            first_ref[i * 8 : i * 8 + 8, :] = best if t == r else jnp.maximum(first_ref[i * 8 : i * 8 + 8, :], best)
+            eight = slice(i * 8, i * 8 + 8)
+            first_ref[eight, :] = best if t == r else jnp.maximum(first_ref[eight, :], best)
         if m + 1 == len(tiles) or tiles[m + 1][0] != r:
             top = jnp.max(first_ref[...], axis=1, keepdims=True)
             result = jnp.where(lane == r, top * scale_ref[own, :], result)
@@ -178,11 +210,19 @@
     out_ref[...] = result[:, :OWN_CAP]
 
 
-def pick_kernel(r_ref, slot_ref, out_ref):
-    slot = slot_ref[...]
-    value = jnp.zeros(slot.shape, f32)
-    for q in range(OWN_CAP):
-        value = jnp.where(slot == q, r_ref[:, q : q + 1], value)
+def pick_kernel(r_ref, named_ref, rank_ref, out_ref):
+    owners, rows = named_ref.shape
+    padded = jnp.concatenate([r_ref[...], jnp.zeros((owners, LANES - r_ref.shape[1]), f32)], axis=1)
+    rest = padded.T[:8, :]
+    pieces = []
+    for _ in range(3):
+        pieces.append(rest.astype(bf16).astype(f32))
+        rest = rest - pieces[-1]
+    found = jnp.dot(
+        jnp.concatenate(pieces, axis=0).astype(bf16), named_ref[...], preferred_element_type=f32
+    )
+    value = found[:8] + found[8:16] + found[16:]
+    value = jnp.where(iota((8, rows), 0) == rank_ref[...], value, 0.0)
     out_ref[...] = jnp.sum(value, axis=0, keepdims=True)
 
 
@@ -208,11 +248,12 @@
     height = owners * (OWN_CAP * width // LANES + META)
     slots = owners * OWN_CAP
     wide = pltpu.VMEM((height, LANES), f32)
-    packed, slot = call(
+    packed, named, rank = call(
         functools.partial(pack_kernel, label_span),
         (
             jax.ShapeDtypeStruct((height, LANES), bf16),
-            jax.ShapeDtypeStruct((owners, rows), f32),
+            jax.ShapeDtypeStruct((owners, rows), bf16),
+            jax.ShapeDtypeStruct((1, rows), jnp.int32),
         ),
         [
             wide,
@@ -221,6 +262,7 @@
             pltpu.VMEM((rows, width), bf16),
             pltpu.SemaphoreType.DMA((2 + X_PIECES,)),
             pltpu.VMEM((slots, rows), bf16),
+            pltpu.VMEM((owners, rows), f32),
         ],
         "pack",
         in_specs=[pl.BlockSpec(memory_space=pltpu.HBM)] * 3,
@@ -248,7 +290,7 @@
         "score",
     )(arrived)
     returned = lax.all_to_all(result, ("gx", "gy"), split_axis=0, concat_axis=0, tiled=True)
-    best = call(pick_kernel, jax.ShapeDtypeStruct((1, rows), f32), [], "pick")(returned, slot)
+    best = call(pick_kernel, jax.ShapeDtypeStruct((1, rows), f32), [], "pick")(returned, named, rank)
     return best.reshape(rows)
 
 

time: 106 us -> 106 us (level)
  no operation moved by 1% of the time
where the time goes in v4:
time: 106 us
  blocking collectives  96.4 us (91%)
  Pallas kernels  9.17 us (9%)
    all_to_all x1, blocking collectives, shards(): lax.all_to_all(packed.reshape(owners, height // owners // 2, 2, LANES), (...  77 us
    all_to_all x1, blocking collectives, shards(): lax.all_to_all(result, ('gx', 'gy'), split_axis=0, concat_axis=0, tiled=T...  19.3 us
    pallas_call x1, Pallas kernels, shards(): call(functools.partial(pack_kernel, label_span), (jax.ShapeDtypeStruct((h...  4.4 us
    pallas_call x1, Pallas kernels, shards(): call(functools.partial(score_kernel, label_span), jax.ShapeDtypeStruct((o...  3.92 us

profile of v4, /device:TPU:1, one launch (start us, length us, event | category | flops | bytes accessed | tf_op | source)
XLA Modules:
  0.0 105.6 jit_solution(12343537819081091672)
XLA Ops:
  0.0 4.4 %pack.1 = (bf16[9728,128]{1,0:T(8,128)(2,1)S(1)}, bf16[256,1024]{1,0:T(8,128)(2,1)S(1)}, s32[1,1024]{1,0:T(1,128)S(1)}) custom-call(s32[1,1024]{1,0:T(1,128)} %bitcast.13, s32[1,1024]{1,0:T(1,128)} %bitcast.14, bf16[1024,768]{1,0:T(8,128)(2,1)} %x_hbm.1), custom_call_target="tpu_custom_call" | custom-call | tf_op jit(solution)/shard_map/pack/pallas_call | solution.py:251
  4.4 77.0 %all_to_all.16 = bf16[256,19,2,128]{3,2,1,0:T(2,128)(2,1)S(1)} all-to-all(bf16[256,19,2,128]{3,2,1,0:T(2,128)(2,1)S(1)} %bitcast.10), channel_id=1, replica_groups=mesh['gx'=64,'gy'=4] {'gx','gy'}, dimensions={0} | all-to-all | bytes 4980736 | tf_op jit(solution)/shard_map/all_to_all | solution.py:270
  81.4 3.9 %score.1 = f32[256,6]{1,0:T(8,128)S(1)} custom-call(bf16[9728,128]{1,0:T(8,128)(2,1)S(1)} %bitcast.9), custom_call_target="tpu_custom_call" | custom-call | tf_op jit(solution)/shard_map/score/pallas_call | solution.py:277
  85.4 19.3 %all_to_all.17 = f32[256,1,6]{2,1,0:T(1,128)S(1)} all-to-all(f32[256,1,6]{2,1,0:T(1,128)S(1)} %bitcast.11), channel_id=1, replica_groups=mesh['gx'=64,'gy'=4] {'gx','gy'}, dimensions={0} | all-to-all | bytes 12288 | tf_op jit(solution)/shard_map/all_to_all | solution.py:292
  104.7 0.8 pick.1

commit v5 on v4

--- a/solution.py
+++ b/solution.py
@@ -44,7 +44,7 @@
     width = x_ref.shape[1]
     parts = width // LANES
     stride = w_ref.shape[0] // owners
-    block = min(256, rows)
+    block = min(512, rows)
     copies = [
         pltpu.make_async_copy(c_hbm, c_ref, sems.at[0]),
         pltpu.make_async_copy(p_hbm, p_ref, sems.at[1]),
@@ -61,19 +61,17 @@
     clusters = c_ref[...]
     owner = clusters // CLUS_DEV
     key = (clusters % CLUS_DEV) * label_span + p_ref[...] + 1
-    ones = jnp.ones((block, block), bf16)
-    earlier = None
+    carry = jnp.zeros((owners, 1), f32)
     for b in range(rows // block):
         cols = slice(b * block, (b + 1) * block)
         named = iota((owners, block), 0) == owner[:, cols]
-        count = named.astype(f32).astype(bf16)
-        rank = jnp.dot(count, before, preferred_element_type=f32)
-        if b:
-            rank = rank + jnp.dot(earlier, ones, preferred_element_type=f32)
-        earlier = earlier + count if b else count
+        count = named.astype(f32)
+        rank = jnp.dot(count.astype(bf16), before, preferred_element_type=f32) + carry
+        carry = carry + jnp.sum(count, axis=1, keepdims=True)
         slot_ref[:, cols] = jnp.where(named, rank, -1.0)
-        named_ref[:, cols] = count
-        rank_ref[:, cols] = jnp.sum(jnp.where(named, rank, 0.0), axis=0, keepdims=True).astype(jnp.int32)
+        named_ref[:, cols] = count.astype(bf16)
+        place = jnp.sum(jnp.where(named, rank, 0.0), axis=0, keepdims=True)
+        rank_ref[:, cols] = place.astype(jnp.int32)
     key = key.astype(f32)
     lane = iota((owners, LANES), 1)
     for copy in copies[2:]:

time: 106 us -> 106 us (level)
  no operation moved by 1% of the time
where the time goes in v5:
time: 106 us
  blocking collectives  96.4 us (91%)
  Pallas kernels  9.17 us (9%)
    all_to_all x1, blocking collectives, shards(): lax.all_to_all(packed.reshape(owners, height // owners // 2, 2, LANES), (...  77 us
    all_to_all x1, blocking collectives, shards(): lax.all_to_all(result, ('gx', 'gy'), split_axis=0, concat_axis=0, tiled=T...  19.3 us
    pallas_call x1, Pallas kernels, shards(): call(functools.partial(pack_kernel, label_span), (jax.ShapeDtypeStruct((h...  4.4 us
    pallas_call x1, Pallas kernels, shards(): call(functools.partial(score_kernel, label_span), jax.ShapeDtypeStruct((o...  3.92 us

profile of v5, /device:TPU:1, one launch (start us, length us, event | category | flops | bytes accessed | tf_op | source)
XLA Modules:
  0.0 105.6 jit_solution(17800743421833190915)
XLA Ops:
  0.0 4.4 %pack.1 = (bf16[9728,128]{1,0:T(8,128)(2,1)S(1)}, bf16[256,1024]{1,0:T(8,128)(2,1)S(1)}, s32[1,1024]{1,0:T(1,128)S(1)}) custom-call(s32[1,1024]{1,0:T(1,128)} %bitcast.13, s32[1,1024]{1,0:T(1,128)} %bitcast.14, bf16[1024,768]{1,0:T(8,128)(2,1)} %x_hbm.1), custom_call_target="tpu_custom_call" | custom-call | tf_op jit(solution)/shard_map/pack/pallas_call | solution.py:249
  4.4 77.0 %all_to_all.16 = bf16[256,19,2,128]{3,2,1,0:T(2,128)(2,1)S(1)} all-to-all(bf16[256,19,2,128]{3,2,1,0:T(2,128)(2,1)S(1)} %bitcast.10), channel_id=1, replica_groups=mesh['gx'=64,'gy'=4] {'gx','gy'}, dimensions={0} | all-to-all | bytes 4980736 | tf_op jit(solution)/shard_map/all_to_all | solution.py:268
  81.4 3.9 %score.1 = f32[256,6]{1,0:T(8,128)S(1)} custom-call(bf16[9728,128]{1,0:T(8,128)(2,1)S(1)} %bitcast.9), custom_call_target="tpu_custom_call" | custom-call | tf_op jit(solution)/shard_map/score/pallas_call | solution.py:275
  85.4 19.3 %all_to_all.17 = f32[256,1,6]{2,1,0:T(1,128)S(1)} all-to-all(f32[256,1,6]{2,1,0:T(1,128)S(1)} %bitcast.11), channel_id=1, replica_groups=mesh['gx'=64,'gy'=4] {'gx','gy'}, dimensions={0} | all-to-all | bytes 12288 | tf_op jit(solution)/shard_map/all_to_all | solution.py:290
  104.7 0.8 pick.1

commit v6 on v5

--- a/solution.py
+++ b/solution.py
@@ -5,11 +5,15 @@
 from jax import lax
 from jax.experimental import pallas as pl
 from jax.experimental.pallas import tpu as pltpu
+from jax.sharding import Mesh
 from jax.sharding import PartitionSpec as P
 
 CLUS_DEV = 2
 OWN_CAP = 6
 LANES = 128
+AXES = ("z", "x", "core", "gy")
+PLACE = (4, 2)
+ORDER = ("core", "x", "gy", "z")
 META = 2
 DIGIT = 128
 X_PIECES = 1
@@ -241,7 +245,7 @@
 
 def shards(embeddings, clusters, priorities):
     rows, width = embeddings.shape
-    owners = lax.axis_size("gx") * lax.axis_size("gy")
+    owners = lax.axis_size(ORDER)
     label_span = rows * owners
     height = owners * (OWN_CAP * width // LANES + META)
     slots = owners * OWN_CAP
@@ -267,7 +271,7 @@
     )(stay(clusters.reshape(1, rows)), stay(priorities.reshape(1, rows)), stay(embeddings))
     arrived = lax.all_to_all(
         packed.reshape(owners, height // owners // 2, 2, LANES),
-        ("gx", "gy"),
+        ORDER,
         split_axis=0,
         concat_axis=0,
         tiled=True,
@@ -287,12 +291,12 @@
         ],
         "score",
     )(arrived)
-    returned = lax.all_to_all(result, ("gx", "gy"), split_axis=0, concat_axis=0, tiled=True)
+    returned = lax.all_to_all(result, ORDER, split_axis=0, concat_axis=0, tiled=True)
     best = call(pick_kernel, jax.ShapeDtypeStruct((1, rows), f32), [], "pick")(returned, named, rank)
     return best.reshape(rows)
 
 
 def solution(mesh):
-    in_specs = (P(("gx", "gy"), None), P(("gx", "gy")), P(("gx", "gy")))
-    out_specs = P(("gx", "gy"))
-    return jax.shard_map(shards, mesh=mesh, in_specs=in_specs, out_specs=out_specs, check_vma=False)
+    fine = Mesh(mesh.devices.reshape(-1, *PLACE, mesh.shape["gy"]), AXES)
+    in_specs = (P(AXES, None), P(AXES), P(AXES))
+    return jax.shard_map(shards, mesh=fine, in_specs=in_specs, out_specs=P(AXES), check_vma=False)

time: 106 us -> 106 us (level)
  no operation moved by 1% of the time
where the time goes in v6:
time: 106 us; the launch traced here: 105 us
  blocking collectives  96.2 us (91%)
  Pallas kernels  9.17 us (9%)
    all_to_all x1, blocking collectives, shards(): lax.all_to_all(packed.reshape(owners, height // owners // 2, 2, LANES), O...  77.3 us
    all_to_all x1, blocking collectives, shards(): lax.all_to_all(result, ORDER, split_axis=0, concat_axis=0, tiled=True)  18.8 us
    pallas_call x1, Pallas kernels, shards(): call(functools.partial(pack_kernel, label_span), (jax.ShapeDtypeStruct((h...  4.4 us
    pallas_call x1, Pallas kernels, shards(): call(functools.partial(score_kernel, label_span), jax.ShapeDtypeStruct((o...  3.92 us

profile of v6, /device:TPU:1, one launch (start us, length us, event | category | flops | bytes accessed | tf_op | source)
XLA Modules:
  0.0 105.4 jit_solution(11449273998693288510)
XLA Ops:
  0.0 4.4 %pack.1 = (bf16[9728,128]{1,0:T(8,128)(2,1)S(1)}, bf16[256,1024]{1,0:T(8,128)(2,1)S(1)}, s32[1,1024]{1,0:T(1,128)S(1)}) custom-call(s32[1,1024]{1,0:T(1,128)} %bitcast.13, s32[1,1024]{1,0:T(1,128)} %bitcast.14, bf16[1024,768]{1,0:T(8,128)(2,1)} %x_hbm.1), custom_call_target="tpu_custom_call" | custom-call | tf_op jit(solution)/shard_map/pack/pallas_call | solution.py:253
  4.4 77.3 %all_to_all.16 = bf16[256,19,2,128]{3,2,1,0:T(2,128)(2,1)S(1)} all-to-all(bf16[256,19,2,128]{3,2,1,0:T(2,128)(2,1)S(1)} %bitcast.10), channel_id=1, replica_groups=mesh['z'=8,'x'=4,'core'=2,'gy'=4] {'core','x','gy','z'}, dimensions={0} | all-to-all | bytes 4980736 | tf_op jit(solution)/shard_map/all_to_all | solution.py:272
  81.8 3.9 %score.1 = f32[256,6]{1,0:T(8,128)S(1)} custom-call(bf16[9728,128]{1,0:T(8,128)(2,1)S(1)} %bitcast.9), custom_call_target="tpu_custom_call" | custom-call | tf_op jit(solution)/shard_map/score/pallas_call | solution.py:279
  85.7 18.8 %all_to_all.17 = f32[256,1,6]{2,1,0:T(1,128)S(1)} all-to-all(f32[256,1,6]{2,1,0:T(1,128)S(1)} %bitcast.11), channel_id=1, replica_groups=mesh['z'=8,'x'=4,'core'=2,'gy'=4] {'core','x','gy','z'}, dimensions={0} | all-to-all | bytes 12288 | tf_op jit(solution)/shard_map/all_to_all | solution.py:294
  104.5 0.8 pick.1

commit v7 on v6

--- a/solution.py
+++ b/solution.py
@@ -14,6 +14,7 @@
 AXES = ("z", "x", "core", "gy")
 PLACE = (4, 2)
 ORDER = ("core", "x", "gy", "z")
+BACK = ("z", "core", "x", "gy")
 META = 2
 DIGIT = 128
 X_PIECES = 1
@@ -30,6 +31,7 @@
 
 def pack_kernel(
     label_span,
+    depth,
     c_hbm,
     p_hbm,
     x_hbm,
@@ -73,7 +75,9 @@
         rank = jnp.dot(count.astype(bf16), before, preferred_element_type=f32) + carry
         carry = carry + jnp.sum(count, axis=1, keepdims=True)
         slot_ref[:, cols] = jnp.where(named, rank, -1.0)
-        named_ref[:, cols] = count.astype(bf16)
+        turn = iota((owners, block), 0)
+        turn = turn % (owners // depth) * depth + turn // (owners // depth)
+        named_ref[:, cols] = (turn == owner[:, cols]).astype(f32).astype(bf16)
         place = jnp.sum(jnp.where(named, rank, 0.0), axis=0, keepdims=True)
         rank_ref[:, cols] = place.astype(jnp.int32)
     key = key.astype(f32)
@@ -119,6 +123,7 @@
 
 def score_kernel(
     label_span,
+    depth,
     w_ref,
     out_ref,
     wide_ref,
@@ -209,7 +214,11 @@
         tops = jnp.where(iota((8, sources), 0) == t, top, tops)
     turned_ref[:8, :] = tops
     result = jnp.maximum(jnp.maximum(result, turned_ref[...].T), -1.0)
-    out_ref[...] = result[:, :OWN_CAP]
+    first_ref[...] = result
+    plane = sources // depth
+    for z in range(depth):
+        part = first_ref[pl.ds(z, plane, stride=depth), :]
+        out_ref[z * plane : (z + 1) * plane, :] = part[:, :OWN_CAP]
 
 
 def pick_kernel(r_ref, named_ref, rank_ref, out_ref):
@@ -246,12 +255,13 @@
 def shards(embeddings, clusters, priorities):
     rows, width = embeddings.shape
     owners = lax.axis_size(ORDER)
+    depth = lax.axis_size("z")
     label_span = rows * owners
     height = owners * (OWN_CAP * width // LANES + META)
     slots = owners * OWN_CAP
     wide = pltpu.VMEM((height, LANES), f32)
     packed, named, rank = call(
-        functools.partial(pack_kernel, label_span),
+        functools.partial(pack_kernel, label_span, depth),
         (
             jax.ShapeDtypeStruct((height, LANES), bf16),
             jax.ShapeDtypeStruct((owners, rows), bf16),
@@ -277,7 +287,7 @@
         tiled=True,
     ).reshape(height, LANES)
     result = call(
-        functools.partial(score_kernel, label_span),
+        functools.partial(score_kernel, label_span, depth),
         jax.ShapeDtypeStruct((owners, OWN_CAP), f32),
         [
             wide,
@@ -291,7 +301,7 @@
         ],
         "score",
     )(arrived)
-    returned = lax.all_to_all(result, ORDER, split_axis=0, concat_axis=0, tiled=True)
+    returned = lax.all_to_all(result, BACK, split_axis=0, concat_axis=0, tiled=True)
     best = call(pick_kernel, jax.ShapeDtypeStruct((1, rows), f32), [], "pick")(returned, named, rank)
     return best.reshape(rows)
 

time: 106 us -> 106 us (level)
  no operation moved by 1% of the time
where the time goes in v7:
time: 106 us
  blocking collectives  96.3 us (91%)
  Pallas kernels  9.16 us (9%)
    all_to_all x1, blocking collectives, shards(): lax.all_to_all(packed.reshape(owners, height // owners // 2, 2, LANES), O...  77.3 us
    all_to_all x1, blocking collectives, shards(): lax.all_to_all(result, BACK, split_axis=0, concat_axis=0, tiled=True)  19 us
    pallas_call x1, Pallas kernels, shards(): call(functools.partial(pack_kernel, label_span, depth), (jax.ShapeDtypeSt...  4.4 us
    pallas_call x1, Pallas kernels, shards(): call(functools.partial(score_kernel, label_span, depth), jax.ShapeDtypeSt...  3.92 us

profile of v7, /device:TPU:1, one launch (start us, length us, event | category | flops | bytes accessed | tf_op | source)
XLA Modules:
  0.0 105.5 jit_solution(5940446583142643829)
XLA Ops:
  0.0 4.4 %pack.1 = (bf16[9728,128]{1,0:T(8,128)(2,1)S(1)}, bf16[256,1024]{1,0:T(8,128)(2,1)S(1)}, s32[1,1024]{1,0:T(1,128)S(1)}) custom-call(s32[1,1024]{1,0:T(1,128)} %bitcast.13, s32[1,1024]{1,0:T(1,128)} %bitcast.14, bf16[1024,768]{1,0:T(8,128)(2,1)} %x_hbm.1), custom_call_target="tpu_custom_call" | custom-call | tf_op jit(solution)/shard_map/pack/pallas_call | solution.py:263
  4.4 77.3 %all_to_all.16 = bf16[256,19,2,128]{3,2,1,0:T(2,128)(2,1)S(1)} all-to-all(bf16[256,19,2,128]{3,2,1,0:T(2,128)(2,1)S(1)} %bitcast.10), channel_id=1, replica_groups=mesh['z'=8,'x'=4,'core'=2,'gy'=4] {'core','x','gy','z'}, dimensions={0} | all-to-all | bytes 4980736 | tf_op jit(solution)/shard_map/all_to_all | solution.py:282
  81.8 3.9 %score.1 = f32[256,6]{1,0:T(8,128)S(1)} custom-call(bf16[9728,128]{1,0:T(8,128)(2,1)S(1)} %bitcast.9), custom_call_target="tpu_custom_call" | custom-call | tf_op jit(solution)/shard_map/score/pallas_call | solution.py:289
  85.7 19.0 %all_to_all.17 = f32[256,1,6]{2,1,0:T(1,128)S(1)} all-to-all(f32[256,1,6]{2,1,0:T(1,128)S(1)} %bitcast.11), channel_id=1, replica_groups=mesh['z'=8,'x'=4,'core'=2,'gy'=4] {'z','core','x','gy'}, dimensions={0} | all-to-all | bytes 12288 | tf_op jit(solution)/shard_map/all_to_all | solution.py:304
  104.7 0.8 pick.1

commit v8 on v5

--- a/solution.py
+++ b/solution.py
@@ -153,52 +153,52 @@
     halves = sources // LANES
     second = [[jnp.full((8, LANES), minus, f32)] * halves for _ in range(OWN_CAP)]
     first = {}
-    tiles = [(r, t) for r in range(OWN_CAP) for t in [r, *range(r)]]
-    for m, (r, t) in enumerate(tiles):
+    spans = [slice(h * LANES, (h + 1) * LANES) for h in range(halves)]
+    for r in range(OWN_CAP):
         own = slice(r * sources, (r + 1) * sources)
-        if t == r:
-            for k in range(parts):
-                x_ref[own, k * LANES : (k + 1) * LANES] = wide_ref[
-                    pl.ds(r * parts + k, sources, stride=stride), :
-                ].astype(bf16)
-        tile_ref[m] = lax.dot_general(
-            x_ref[own, :],
-            x_ref[t * sources : (t + 1) * sources, :],
-            (((1,), (1,)), ((), ())),
-            preferred_element_type=f32,
-        )
-        if t == r:
-            squares = jnp.where(here, tile_ref[m], 0.0)
-            scale = lax.rsqrt(jnp.sum(squares, axis=1, keepdims=True) + norm_eps)
-            scale_ref[own, :] = jnp.broadcast_to(scale, (sources, LANES))
-            turned_ref[16 + r : 17 + r, :] = lax.rsqrt(
-                jnp.sum(squares, axis=0, keepdims=True) + norm_eps
+        for k in range(parts):
+            x_ref[own, k * LANES : (k + 1) * LANES] = wide_ref[
+                pl.ds(r * parts + k, sources, stride=stride), :
+            ].astype(bf16)
+        order = [r, *range(r)]
+        for t in order:
+            tile_ref[t] = lax.dot_general(
+                x_ref[own, :],
+                x_ref[t * sources : (t + 1) * sources, :],
+                (((1,), (1,)), ((), ())),
+                preferred_element_type=f32,
             )
-        spans = [slice(h * LANES, (h + 1) * LANES) for h in range(halves)]
-        label_row = [jnp.broadcast_to(turned_ref[8 + t : 9 + t, c], (8, LANES)) for c in spans]
-        key_row = [jnp.broadcast_to(turned_ref[t : t + 1, c], (8, LANES)) for c in spans]
-        scale_row = [jnp.broadcast_to(turned_ref[16 + t : 17 + t, c], (8, LANES)) for c in spans]
-        for i in range(sources // 8):
-            at = slice(r * sources + i * 8, r * sources + i * 8 + 8)
-            label_col, key_col = label_ref[at, :], key_ref[at, :]
-            if t != r:
-                scale_col = scale_ref[at, :]
-            forwards = []
-            for h in range(halves):
-                score = tile_ref[m, i * 8 : (i + 1) * 8, spans[h]]
-                score = jnp.where(label_col == label_row[h], score, minus)
-                later = key_row[h] < key_col
-                forward = jnp.where(later, score * scale_row[h], minus)
-                forwards.append(forward)
-                if t != r:
-                    back = jnp.where(later, minus, score * scale_col)
-                    second[t][h] = jnp.maximum(second[t][h], back)
-            best = jnp.maximum(*forwards)
-            eight = slice(i * 8, i * 8 + 8)
-            first_ref[eight, :] = best if t == r else jnp.maximum(first_ref[eight, :], best)
-        if m + 1 == len(tiles) or tiles[m + 1][0] != r:
-            top = jnp.max(first_ref[...], axis=1, keepdims=True)
-            result = jnp.where(lane == r, top * scale_ref[own, :], result)
+            if t == r:
+                squares = jnp.where(here, tile_ref[t], 0.0)
+                scale = lax.rsqrt(jnp.sum(squares, axis=1, keepdims=True) + norm_eps)
+                scale_ref[own, :] = jnp.broadcast_to(scale, (sources, LANES))
+                turned_ref[16 + r : 17 + r, :] = lax.rsqrt(
+                    jnp.sum(squares, axis=0, keepdims=True) + norm_eps
+                )
+        for i in range(0, sources, 32):
+            subs = [slice(r * sources + i + j, r * sources + i + j + 8) for j in range(0, 32, 8)]
+            label_col = [label_ref[at, :] for at in subs]
+            key_col = [key_ref[at, :] for at in subs]
+            scale_col = [scale_ref[at, :] for at in subs]
+            best = [None] * len(subs)
+            for t in order:
+                for h, c in enumerate(spans):
+                    key_row = jnp.broadcast_to(turned_ref[t : t + 1, c], (8, LANES))
+                    label_row = jnp.broadcast_to(turned_ref[8 + t : 9 + t, c], (8, LANES))
+                    scale_row = jnp.broadcast_to(turned_ref[16 + t : 17 + t, c], (8, LANES))
+                    for j in range(len(subs)):
+                        score = tile_ref[t, i + 8 * j : i + 8 * j + 8, c]
+                        score = jnp.where(label_col[j] == label_row, score, minus)
+                        later = key_row < key_col[j]
+                        forward = jnp.where(later, score * scale_row, minus)
+                        best[j] = forward if best[j] is None else jnp.maximum(best[j], forward)
+                        if t != r:
+                            back = jnp.where(later, minus, score * scale_col[j])
+                            second[t][h] = jnp.maximum(second[t][h], back)
+            for j in range(len(subs)):
+                first_ref[i + 8 * j : i + 8 * j + 8, :] = best[j]
+        top = jnp.max(first_ref[...], axis=1, keepdims=True)
+        result = jnp.where(lane == r, top * scale_ref[own, :], result)
     for t in range(OWN_CAP):
         top = jnp.concatenate([jnp.max(s, axis=0, keepdims=True) for s in second[t]], axis=1)
         top = top * turned_ref[16 + t : 17 + t, :]

time: 106 us -> 106 us (level)
  no operation moved by 1% of the time
where the time goes in v8:
time: 106 us
  blocking collectives  96.4 us (91%)
  Pallas kernels  9.13 us (9%)
    all_to_all x1, blocking collectives, shards(): lax.all_to_all(packed.reshape(owners, height // owners // 2, 2, LANES), (...  77 us
    all_to_all x1, blocking collectives, shards(): lax.all_to_all(result, ('gx', 'gy'), split_axis=0, concat_axis=0, tiled=T...  19.3 us
    pallas_call x1, Pallas kernels, shards(): call(functools.partial(pack_kernel, label_span), (jax.ShapeDtypeStruct((h...  4.4 us
    pallas_call x1, Pallas kernels, shards(): call(functools.partial(score_kernel, label_span), jax.ShapeDtypeStruct((o...  3.88 us

profile of v8, /device:TPU:1, one launch (start us, length us, event | category | flops | bytes accessed | tf_op | source)
XLA Modules:
  0.0 105.5 jit_solution(11941687826400954702)
XLA Ops:
  0.0 4.4 %pack.1 = (bf16[9728,128]{1,0:T(8,128)(2,1)S(1)}, bf16[256,1024]{1,0:T(8,128)(2,1)S(1)}, s32[1,1024]{1,0:T(1,128)S(1)}) custom-call(s32[1,1024]{1,0:T(1,128)} %bitcast.13, s32[1,1024]{1,0:T(1,128)} %bitcast.14, bf16[1024,768]{1,0:T(8,128)(2,1)} %x_hbm.1), custom_call_target="tpu_custom_call" | custom-call | tf_op jit(solution)/shard_map/pack/pallas_call | solution.py:249
  4.4 77.0 %all_to_all.16 = bf16[256,19,2,128]{3,2,1,0:T(2,128)(2,1)S(1)} all-to-all(bf16[256,19,2,128]{3,2,1,0:T(2,128)(2,1)S(1)} %bitcast.10), channel_id=1, replica_groups=mesh['gx'=64,'gy'=4] {'gx','gy'}, dimensions={0} | all-to-all | bytes 4980736 | tf_op jit(solution)/shard_map/all_to_all | solution.py:268
  81.4 3.9 %score.1 = f32[256,6]{1,0:T(8,128)S(1)} custom-call(bf16[9728,128]{1,0:T(8,128)(2,1)S(1)} %bitcast.9), custom_call_target="tpu_custom_call" | custom-call | tf_op jit(solution)/shard_map/score/pallas_call | solution.py:275
  85.3 19.3 %all_to_all.17 = f32[256,1,6]{2,1,0:T(1,128)S(1)} all-to-all(f32[256,1,6]{2,1,0:T(1,128)S(1)} %bitcast.11), channel_id=1, replica_groups=mesh['gx'=64,'gy'=4] {'gx','gy'}, dimensions={0} | all-to-all | bytes 12288 | tf_op jit(solution)/shard_map/all_to_all | solution.py:290
  104.7 0.8 pick.1

commit v9 on v6

--- a/solution.py
+++ b/solution.py
@@ -13,7 +13,7 @@
 LANES = 128
 AXES = ("z", "x", "core", "gy")
 PLACE = (4, 2)
-ORDER = ("core", "x", "gy", "z")
+ORDER = ("core", "gy", "z", "x")
 META = 2
 DIGIT = 128
 X_PIECES = 1

time: 106 us -> 105 us (level)
  no operation moved by 1% of the time
where the time goes in v9:
time: 105 us
  blocking collectives  95.9 us (91%)
  Pallas kernels  9.17 us (9%)
    all_to_all x1, blocking collectives, shards(): lax.all_to_all(packed.reshape(owners, height // owners // 2, 2, LANES), O...  76.5 us
    all_to_all x1, blocking collectives, shards(): lax.all_to_all(result, ORDER, split_axis=0, concat_axis=0, tiled=True)  19.4 us
    pallas_call x1, Pallas kernels, shards(): call(functools.partial(pack_kernel, label_span), (jax.ShapeDtypeStruct((h...  4.4 us
    pallas_call x1, Pallas kernels, shards(): call(functools.partial(score_kernel, label_span), jax.ShapeDtypeStruct((o...  3.92 us

profile of v9, /device:TPU:1, one launch (start us, length us, event | category | flops | bytes accessed | tf_op | source)
XLA Modules:
  0.0 105.1 jit_solution(17359415152545233698)
XLA Ops:
  0.0 4.4 %pack.1 = (bf16[9728,128]{1,0:T(8,128)(2,1)S(1)}, bf16[256,1024]{1,0:T(8,128)(2,1)S(1)}, s32[1,1024]{1,0:T(1,128)S(1)}) custom-call(s32[1,1024]{1,0:T(1,128)} %bitcast.13, s32[1,1024]{1,0:T(1,128)} %bitcast.14, bf16[1024,768]{1,0:T(8,128)(2,1)} %x_hbm.1), custom_call_target="tpu_custom_call" | custom-call | tf_op jit(solution)/shard_map/pack/pallas_call | solution.py:253
  4.4 76.5 %all_to_all.16 = bf16[256,19,2,128]{3,2,1,0:T(2,128)(2,1)S(1)} all-to-all(bf16[256,19,2,128]{3,2,1,0:T(2,128)(2,1)S(1)} %bitcast.10), channel_id=1, replica_groups=mesh['z'=8,'x'=4,'core'=2,'gy'=4] {'core','gy','z','x'}, dimensions={0} | all-to-all | bytes 4980736 | tf_op jit(solution)/shard_map/all_to_all | solution.py:272
  80.9 3.9 %score.1 = f32[256,6]{1,0:T(8,128)S(1)} custom-call(bf16[9728,128]{1,0:T(8,128)(2,1)S(1)} %bitcast.9), custom_call_target="tpu_custom_call" | custom-call | tf_op jit(solution)/shard_map/score/pallas_call | solution.py:279
  84.8 19.4 %all_to_all.17 = f32[256,1,6]{2,1,0:T(1,128)S(1)} all-to-all(f32[256,1,6]{2,1,0:T(1,128)S(1)} %bitcast.11), channel_id=1, replica_groups=mesh['z'=8,'x'=4,'core'=2,'gy'=4] {'core','gy','z','x'}, dimensions={0} | all-to-all | bytes 12288 | tf_op jit(solution)/shard_map/all_to_all | solution.py:294
  104.3 0.8 pick.1
